TPU v7x, 32 devices: a whole 2x2x4 slice. The times are simulated.
32 devices in a mesh: tm: 4 (over y, x), space: 8 (over z, core).
Axes of the slice: x: 2, y: 2, z: 4, core: 2. Of those that a mesh axis runs over, the one named last changes fastest.
Arguments:
- state: float32 [4, 64, 32, 256], P('tm', 'space'), may hold values from -2 to 2
- initial: float32 [64, 32, 256], P('space'), may hold values from -2.5 to 2.5
- labels: int32 [64, 32, 256], P('space'), may hold values from 0 to 15
- mobility_table: float32 [16], replicated, may hold values from 0.5 to 2
Outputs:
- new_state: float32 [4, 64, 32, 256], P('tm', 'space')
All inputs are finite; a program needn't handle non-finite values.
Results may differ from a plain program's by a relative error of at most 0.0003.
Values sent between devices are 32-bit elements; how exact they have to be, the bound alone decides.
A program may use at most 64 MiB of HBM per device.

v0:
```python
import math

import jax
import jax.numpy as jnp
from jax import lax
from jax.sharding import PartitionSpec as P

SWEEPS = 8
GRAINS = 16


alpha_wrap = 0.1
tau_step = 0.25
kappa_grad = 4.0
diag_extra = 6.5


def passed_along(array, axis, by):
    devices = lax.axis_size(axis)
    pairs = [(i, i + by) for i in range(devices) if 0 <= i + by < devices]
    return lax.ppermute(array, axis, pairs)


def extended(cells, sides, width):
    for axis, dim in sides:
        count = lax.axis_size(axis)
        head = lax.slice_in_dim(cells, 0, width, axis=dim)
        tail = lax.slice_in_dim(cells, cells.shape[dim] - width, cells.shape[dim], axis=dim)
        cells = jnp.concatenate(
            [
                lax.ppermute(tail, axis, [(i, (i + 1) % count) for i in range(count)]),
                cells,
                lax.ppermute(head, axis, [((i + 1) % count, i) for i in range(count)]),
            ],
            axis=dim,
        )
    return cells


def partner_2(value, axis, apart):
    mask = 2**apart
    pairs = [(source, source ^ mask) for source in range(lax.axis_size(axis))]
    return lax.ppermute(value, axis, pairs)


def plane_sum(grid_field):
    summed = jnp.roll(grid_field, 1, -2) + jnp.roll(grid_field, -1, -2)
    return summed + jnp.roll(grid_field, 1, -1) + jnp.roll(grid_field, -1, -1)


def mobility_of(labels, rate_table):

    def add_grain(grain_id, summed):
        return summed + jnp.where(
            labels == grain_id, rate_table[grain_id], jnp.zeros((), rate_table.dtype)
        )

    return lax.fori_loop(0, GRAINS, add_grain, jnp.zeros(labels.shape, rate_table.dtype))


def complex_times(left_val, right_val):
    return jnp.stack(
        [
            left_val[0] * right_val[0] - left_val[1] * right_val[1],
            left_val[0] * right_val[1] + left_val[1] * right_val[0],
        ]
    )


def sweep_once(padded, spectral_rhs, inverse_diag, mobility):
    middle = padded[:, 1:-1]
    summed = spectral_rhs + mobility * (padded[:, 2:] + padded[:, :-2] + plane_sum(middle))
    return complex_times(summed, inverse_diag)


def inverse_of(mobility, freq_angle, beta_root):
    diag_real = 1.0 - beta_root * jnp.cos(freq_angle) + diag_extra * mobility
    diag_imag = beta_root * jnp.sin(freq_angle)
    magnitude = diag_real * diag_real + diag_imag * diag_imag
    return jnp.stack([diag_real / magnitude, -diag_imag / magnitude])


def shards(state, initial, labels, mobility_table):
    time_count = lax.axis_size("tm")
    section_count = time_count.bit_length() - 1
    time_index = lax.axis_index("tm")
    index_float = time_index.astype(jnp.float32)
    angle_unit = 2.0 * math.pi / time_count
    gamma_here = alpha_wrap ** (index_float / time_count)
    current = state[0]
    mobility = mobility_of(labels, mobility_table)
    earlier = passed_along(state, "tm", 1)
    earlier_step = jnp.where(time_index == 0, initial, earlier[0])
    padded = extended(current, (("space", 0),), 1)
    laplacian = padded[2:] + padded[:-2] + plane_sum(current) - 6.0 * current
    residual = (
        current
        - earlier_step
        + tau_step * mobility * (current * current * current - current - kappa_grad * laplacian)
    )
    top_bit = section_count - 1
    half_span = 2**top_bit
    local_part = residual * gamma_here
    partner = partner_2(local_part, "tm", top_bit)
    upper_half = time_index // half_span % 2 == 1
    twist_angle = -math.pi * (time_index % half_span).astype(jnp.float32) / half_span
    difference = partner - local_part
    spectral_rhs = jnp.stack(
        [
            jnp.where(upper_half, difference * jnp.cos(twist_angle), local_part + partner),
            jnp.where(upper_half, difference * jnp.sin(twist_angle), jnp.zeros_like(local_part)),
        ]
    )
    for bit_number in range(top_bit - 1, -1, -1):
        half_span = 2**bit_number
        partner = partner_2(spectral_rhs, "tm", bit_number)
        upper_half = time_index // half_span % 2 == 1
        twist_angle = -math.pi * (time_index % half_span).astype(jnp.float32) / half_span
        twiddle = jnp.stack([jnp.cos(twist_angle), jnp.sin(twist_angle)])
        spectral_rhs = jnp.where(
            upper_half, complex_times(partner - spectral_rhs, twiddle), spectral_rhs + partner
        )
    frequency = jnp.zeros((), jnp.int32)
    for bit_number in range(section_count):
        frequency = frequency + time_index // 2**bit_number % 2 * 2 ** (
            section_count - 1 - bit_number
        )
    beta_root = alpha_wrap ** (1.0 / time_count)
    freq_angle = frequency.astype(jnp.float32) * angle_unit
    inverse_diag = inverse_of(mobility, freq_angle, beta_root)
    spectral_sol = complex_times(spectral_rhs, inverse_diag)
    for sweep_index in range(SWEEPS):
        padded_sol = extended(spectral_sol, (("space", 1),), 1)
        spectral_sol = sweep_once(padded_sol, spectral_rhs, inverse_diag, mobility)
    for bit_number in range(section_count):
        half_span = 2**bit_number
        partner = partner_2(spectral_sol, "tm", bit_number)
        upper_half = time_index // half_span % 2 == 1
        twist_angle = math.pi * (time_index % half_span).astype(jnp.float32) / half_span
        twiddle = jnp.stack([jnp.cos(twist_angle), jnp.sin(twist_angle)])
        spectral_sol = jnp.where(
            upper_half,
            partner - complex_times(spectral_sol, twiddle),
            spectral_sol + complex_times(partner, twiddle),
        )
    correction = (spectral_sol[0] / (time_count * gamma_here))[None]
    return state - correction


def solution(mesh):
    in_specs = (P("tm", "space", None, None), P("space", None, None), P("space", None, None), P())
    out_specs = P("tm", "space", None, None)
    return jax.shard_map(shards, mesh=mesh, in_specs=in_specs, out_specs=out_specs, check_vma=False)
```

profile of v0, /device:TPU:0, one launch (start us, length us, event | category | flops | bytes accessed | tf_op | source)
XLA Modules:
  0.0 138.2 jit_solution(828189935546278437)
XLA Ops:
  0.0 4.8 %collective-permute-start = (f32[1,8,32,256]{3,2,1,0:T(8,128)}, f32[1,8,32,256]{3,2,1,0:T(8,128)S(1)}, u32[]{:S(2)}, u32[]{:S(2)}) collective-permute-start(f32[1,8,32,256]{3,2,1,0:T(8,128)} %param.6), channel_id=1, source_target_pairs={{0,8},{8,16},{16,24},{1,9},{9,17},{17,25},{2,10},{10,18},{18,26},{... | collective-permute-start | bytes 786440 | tf_op jit(solution)/shard_map/ppermute | solution.py:21
  4.9 0.8 slice_bitcast_fusion.19
  5.7 2.8 %collective-permute-start.1 = (f32[1,32,256]{2,1,0:T(8,128)S(1)}, f32[1,32,256]{2,1,0:T(8,128)S(1)}, u32[]{:S(2)}, u32[]{:S(2)}) collective-permute-start(f32[1,32,256]{2,1,0:T(8,128)S(1)} %get-tuple-element.209), channel_id=1, source_target_pairs={{1,0},{2,1},{3,2},{4,3},{5,4},{6,5},{7,6},{0,7},{9,8},{10,9},{11,1... | collective-permute-start | bytes 98312 | tf_op jit(solution)/shard_map/ppermute | solution.py:33
  8.4 1.2 fusion.148
  9.7 0.9 copy-done.1
  10.6 23.6 %while.14 = (s32[]{:T(128)}, f32[8,32,256]{2,1,0:T(8,128)S(1)}, s32[8,32,256]{2,1,0:T(8,128)S(1)}, f32[16]{0:T(128)S(1)}, s32[]{:T(128)}, /*index=5*/s32[]{:T(128)}) while((s32[]{:T(128)}, f32[8,32,256]{2,1,0:T(8,128)S(1)}, s32[8,32,256]{2,1,0:T(8,128)S(1)}, f32[16]{0:T(128)S(1)}, s32[]{:T(128)}, /*index=5*/s32[]{:T(128)}) %tuple.88), condition=%wide.region_1.2_spmd.clone, body=%wide.region_0.1_spmd.clone.sunk | while | flops 262147 | bytes 786531 | solution.py:58
  11.3 0.8 select_add_fusion.2
  12.1 0.7 dynamic_slice.9
  12.8 0.8 select_add_fusion.2
  13.6 0.7 dynamic_slice.9
  14.2 0.8 select_add_fusion.2
  15.0 0.7 dynamic_slice.9
  15.7 0.8 select_add_fusion.2
  16.5 0.7 dynamic_slice.9
  17.2 0.8 select_add_fusion.2
  18.0 0.7 dynamic_slice.9
  18.7 0.8 select_add_fusion.2
  19.5 0.7 dynamic_slice.9
  20.1 0.8 select_add_fusion.2
  20.9 0.7 dynamic_slice.9
  21.6 0.8 select_add_fusion.2
  22.4 0.7 dynamic_slice.9
  23.1 0.8 select_add_fusion.2
  23.9 0.7 dynamic_slice.9
  24.5 0.8 select_add_fusion.2
  25.4 0.7 dynamic_slice.9
  26.0 0.8 select_add_fusion.2
  26.8 0.7 dynamic_slice.9
  27.5 0.8 select_add_fusion.2
  28.3 0.7 dynamic_slice.9
  29.0 0.8 select_add_fusion.2
  29.8 0.7 dynamic_slice.9
  30.4 0.8 select_add_fusion.2
  31.2 0.7 dynamic_slice.9
  31.9 0.8 select_add_fusion.2
  33.4 0.8 select_add_fusion.2
  34.4 0.7 copy-done.2
  35.5 1.6 %collective-permute-start.3 = (f32[8,32,256]{2,1,0:T(8,128)S(1)}, f32[8,32,256]{2,1,0:T(8,128)S(1)}, u32[]{:S(2)}, u32[]{:S(2)}) collective-permute-start(f32[8,32,256]{2,1,0:T(8,128)S(1)} %fusion.92), channel_id=1, source_target_pairs={{0,16},{8,24},{16,0},{24,8},{1,17},{9,25},{17,1},{25,9},{2,18},{10... | collective-permute-start | bytes 786440 | tf_op jit(solution)/shard_map/ppermute | solution.py:43
  37.2 5.5 %collective-permute-done.3 = f32[8,32,256]{2,1,0:T(8,128)S(1)} collective-permute-done((f32[8,32,256]{2,1,0:T(8,128)S(1)}, f32[8,32,256]{2,1,0:T(8,128)S(1)}, u32[]{:S(2)}, u32[]{:S(2)}) %collective-permute-start.3) | collective-permute-done | bytes 262176 | tf_op jit(solution)/shard_map/ppermute | solution.py:43
  42.8 1.6 %collective-permute-start.4 = (f32[2,8,32,256]{3,2,1,0:T(8,128)S(1)}, f32[2,8,32,256]{3,2,1,0:T(8,128)S(1)}, u32[]{:S(2)}, u32[]{:S(2)}) collective-permute-start(f32[2,8,32,256]{3,2,1,0:T(8,128)S(1)} %pad_maximum_fusion.40), channel_id=1, source_target_pairs={{0,8},{8,0},{16,24},{24,16},{1,9},{9,1},{17,25},{25,17},{2,10},{10... | collective-permute-start | bytes 1572872 | tf_op jit(solution)/shard_map/ppermute | solution.py:43
  44.6 10.2 %collective-permute-done.4 = f32[2,8,32,256]{3,2,1,0:T(8,128)S(1)} collective-permute-done((f32[2,8,32,256]{3,2,1,0:T(8,128)S(1)}, f32[2,8,32,256]{3,2,1,0:T(8,128)S(1)}, u32[]{:S(2)}, u32[]{:S(2)}) %collective-permute-start.4) | collective-permute-done | bytes 524320 | tf_op jit(solution)/shard_map/ppermute | solution.py:43
  55.6 4.0 %collective-permute-start.5 = (f32[2,1,32,256]{3,2,1,0:T(8,128)S(1)}, f32[2,1,32,256]{3,2,1,0:T(8,128)S(1)}, u32[]{:S(2)}, u32[]{:S(2)}) collective-permute-start(f32[2,1,32,256]{3,2,1,0:T(8,128)S(1)} %get-tuple-element.195), channel_id=1, source_target_pairs={{1,0},{2,1},{3,2},{4,3},{5,4},{6,5},{7,6},{0,7},{9,8},{10,9},{11,1... | collective-permute-start | bytes 196616 | tf_op jit(solution)/shard_map/ppermute | solution.py:33
  59.7 1.9 %collective-permute-done.5 = f32[2,1,32,256]{3,2,1,0:T(8,128)S(1)} collective-permute-done((f32[2,1,32,256]{3,2,1,0:T(8,128)S(1)}, f32[2,1,32,256]{3,2,1,0:T(8,128)S(1)}, u32[]{:S(2)}, u32[]{:S(2)}) %collective-permute-start.5) | collective-permute-done | bytes 65568 | tf_op jit(solution)/shard_map/ppermute | solution.py:33
  61.6 3.6 %collective-permute-done.6 = f32[2,1,32,256]{3,2,1,0:T(8,128)S(1)} collective-permute-done((f32[2,1,32,256]{3,2,1,0:T(8,128)S(1)}, f32[2,1,32,256]{3,2,1,0:T(8,128)S(1)}, u32[]{:S(2)}, u32[]{:S(2)}) %collective-permute-start.6) | collective-permute-done | bytes 65568 | tf_op jit(solution)/shard_map/ppermute | solution.py:31
  66.9 1.8 %collective-permute-done.7 = f32[2,1,32,256]{3,2,1,0:T(8,128)S(1)} collective-permute-done((f32[2,1,32,256]{3,2,1,0:T(8,128)S(1)}, f32[2,1,32,256]{3,2,1,0:T(8,128)S(1)}, u32[]{:S(2)}, u32[]{:S(2)}) %collective-permute-start.7) | collective-permute-done | bytes 65568 | tf_op jit(solution)/shard_map/ppermute | solution.py:33
  68.7 3.2 %collective-permute-done.8 = f32[2,1,32,256]{3,2,1,0:T(8,128)S(1)} collective-permute-done((f32[2,1,32,256]{3,2,1,0:T(8,128)S(1)}, f32[2,1,32,256]{3,2,1,0:T(8,128)S(1)}, u32[]{:S(2)}, u32[]{:S(2)}) %collective-permute-start.8) | collective-permute-done | bytes 65568 | tf_op jit(solution)/shard_map/ppermute | solution.py:31
  73.2 3.5 %collective-permute-start.9 = (f32[2,1,32,256]{3,2,1,0:T(8,128)S(1)}, f32[2,1,32,256]{3,2,1,0:T(8,128)S(1)}, u32[]{:S(2)}, u32[]{:S(2)}) collective-permute-start(f32[2,1,32,256]{3,2,1,0:T(8,128)S(1)} %get-tuple-element.179), channel_id=1, source_target_pairs={{1,0},{2,1},{3,2},{4,3},{5,4},{6,5},{7,6},{0,7},{9,8},{10,9},{11,1... | collective-permute-start | bytes 196616 | tf_op jit(solution)/shard_map/ppermute | solution.py:33
  76.8 2.0 %collective-permute-done.10 = f32[2,1,32,256]{3,2,1,0:T(8,128)S(1)} collective-permute-done((f32[2,1,32,256]{3,2,1,0:T(8,128)S(1)}, f32[2,1,32,256]{3,2,1,0:T(8,128)S(1)}, u32[]{:S(2)}, u32[]{:S(2)}) %collective-permute-start.10) | collective-permute-done | bytes 65568 | tf_op jit(solution)/shard_map/ppermute | solution.py:31
  79.9 3.6 %collective-permute-start.11 = (f32[2,1,32,256]{3,2,1,0:T(8,128)S(1)}, f32[2,1,32,256]{3,2,1,0:T(8,128)S(1)}, u32[]{:S(2)}, u32[]{:S(2)}) collective-permute-start(f32[2,1,32,256]{3,2,1,0:T(8,128)S(1)} %get-tuple-element.171), channel_id=1, source_target_pairs={{1,0},{2,1},{3,2},{4,3},{5,4},{6,5},{7,6},{0,7},{9,8},{10,9},{11,1... | collective-permute-start | bytes 196616 | tf_op jit(solution)/shard_map/ppermute | solution.py:33
  83.5 1.9 %collective-permute-done.11 = f32[2,1,32,256]{3,2,1,0:T(8,128)S(1)} collective-permute-done((f32[2,1,32,256]{3,2,1,0:T(8,128)S(1)}, f32[2,1,32,256]{3,2,1,0:T(8,128)S(1)}, u32[]{:S(2)}, u32[]{:S(2)}) %collective-permute-start.11) | collective-permute-done | bytes 65568 | tf_op jit(solution)/shard_map/ppermute | solution.py:33
  85.4 3.6 %collective-permute-done.12 = f32[2,1,32,256]{3,2,1,0:T(8,128)S(1)} collective-permute-done((f32[2,1,32,256]{3,2,1,0:T(8,128)S(1)}, f32[2,1,32,256]{3,2,1,0:T(8,128)S(1)}, u32[]{:S(2)}, u32[]{:S(2)}) %collective-permute-start.12) | collective-permute-done | bytes 65568 | tf_op jit(solution)/shard_map/ppermute | solution.py:31
  90.8 1.8 %collective-permute-done.13 = f32[2,1,32,256]{3,2,1,0:T(8,128)S(1)} collective-permute-done((f32[2,1,32,256]{3,2,1,0:T(8,128)S(1)}, f32[2,1,32,256]{3,2,1,0:T(8,128)S(1)}, u32[]{:S(2)}, u32[]{:S(2)}) %collective-permute-start.13) | collective-permute-done | bytes 65568 | tf_op jit(solution)/shard_map/ppermute | solution.py:33
  92.6 3.2 %collective-permute-done.14 = f32[2,1,32,256]{3,2,1,0:T(8,128)S(1)} collective-permute-done((f32[2,1,32,256]{3,2,1,0:T(8,128)S(1)}, f32[2,1,32,256]{3,2,1,0:T(8,128)S(1)}, u32[]{:S(2)}, u32[]{:S(2)}) %collective-permute-start.14) | collective-permute-done | bytes 65568 | tf_op jit(solution)/shard_map/ppermute | solution.py:31
  97.7 1.9 %collective-permute-done.15 = f32[2,1,32,256]{3,2,1,0:T(8,128)S(1)} collective-permute-done((f32[2,1,32,256]{3,2,1,0:T(8,128)S(1)}, f32[2,1,32,256]{3,2,1,0:T(8,128)S(1)}, u32[]{:S(2)}, u32[]{:S(2)}) %collective-permute-start.15) | collective-permute-done | bytes 65568 | tf_op jit(solution)/shard_map/ppermute | solution.py:33
  99.6 3.7 %collective-permute-done.16 = f32[2,1,32,256]{3,2,1,0:T(8,128)S(1)} collective-permute-done((f32[2,1,32,256]{3,2,1,0:T(8,128)S(1)}, f32[2,1,32,256]{3,2,1,0:T(8,128)S(1)}, u32[]{:S(2)}, u32[]{:S(2)}) %collective-permute-start.16) | collective-permute-done | bytes 65568 | tf_op jit(solution)/shard_map/ppermute | solution.py:31
  105.0 1.8 %collective-permute-done.17 = f32[2,1,32,256]{3,2,1,0:T(8,128)S(1)} collective-permute-done((f32[2,1,32,256]{3,2,1,0:T(8,128)S(1)}, f32[2,1,32,256]{3,2,1,0:T(8,128)S(1)}, u32[]{:S(2)}, u32[]{:S(2)}) %collective-permute-start.17) | collective-permute-done | bytes 65568 | tf_op jit(solution)/shard_map/ppermute | solution.py:33
  106.8 3.3 %collective-permute-done.18 = f32[2,1,32,256]{3,2,1,0:T(8,128)S(1)} collective-permute-done((f32[2,1,32,256]{3,2,1,0:T(8,128)S(1)}, f32[2,1,32,256]{3,2,1,0:T(8,128)S(1)}, u32[]{:S(2)}, u32[]{:S(2)}) %collective-permute-start.18) | collective-permute-done | bytes 65568 | tf_op jit(solution)/shard_map/ppermute | solution.py:31
  111.9 1.9 %collective-permute-done.19 = f32[2,1,32,256]{3,2,1,0:T(8,128)S(1)} collective-permute-done((f32[2,1,32,256]{3,2,1,0:T(8,128)S(1)}, f32[2,1,32,256]{3,2,1,0:T(8,128)S(1)}, u32[]{:S(2)}, u32[]{:S(2)}) %collective-permute-start.19) | collective-permute-done | bytes 65568 | tf_op jit(solution)/shard_map/ppermute | solution.py:33
  113.7 3.6 %collective-permute-done.20 = f32[2,1,32,256]{3,2,1,0:T(8,128)S(1)} collective-permute-done((f32[2,1,32,256]{3,2,1,0:T(8,128)S(1)}, f32[2,1,32,256]{3,2,1,0:T(8,128)S(1)}, u32[]{:S(2)}, u32[]{:S(2)}) %collective-permute-start.20) | collective-permute-done | bytes 65568 | tf_op jit(solution)/shard_map/ppermute | solution.py:31
  118.1 1.6 %collective-permute-start.21 = (f32[2,8,32,256]{3,2,1,0:T(8,128)S(1)}, f32[2,8,32,256]{3,2,1,0:T(8,128)S(1)}, u32[]{:S(2)}, u32[]{:S(2)}) collective-permute-start(f32[2,8,32,256]{3,2,1,0:T(8,128)S(1)} %pad_maximum_fusion.41), channel_id=1, source_target_pairs={{0,8},{8,0},{16,24},{24,16},{1,9},{9,1},{17,25},{25,17},{2,10},{10... | collective-permute-start | bytes 1572872 | tf_op jit(solution)/shard_map/ppermute | solution.py:43
  119.7 8.2 %collective-permute-done.21 = f32[2,8,32,256]{3,2,1,0:T(8,128)S(1)} collective-permute-done((f32[2,8,32,256]{3,2,1,0:T(8,128)S(1)}, f32[2,8,32,256]{3,2,1,0:T(8,128)S(1)}, u32[]{:S(2)}, u32[]{:S(2)}) %collective-permute-start.21) | collective-permute-done | bytes 524320 | tf_op jit(solution)/shard_map/ppermute | solution.py:43
  128.1 1.6 %collective-permute-start.22 = (f32[2,8,32,256]{3,2,1,0:T(8,128)S(1)}, f32[2,8,32,256]{3,2,1,0:T(8,128)S(1)}, u32[]{:S(2)}, u32[]{:S(2)}) collective-permute-start(f32[2,8,32,256]{3,2,1,0:T(8,128)S(1)} %fusion.88), channel_id=1, source_target_pairs={{0,16},{8,24},{16,0},{24,8},{1,17},{9,25},{17,1},{25,9},{2,18},{10... | collective-permute-start | bytes 1572872 | tf_op jit(solution)/shard_map/ppermute | solution.py:43
  129.9 7.4 %collective-permute-done.22 = f32[2,8,32,256]{3,2,1,0:T(8,128)S(1)} collective-permute-done((f32[2,8,32,256]{3,2,1,0:T(8,128)S(1)}, f32[2,8,32,256]{3,2,1,0:T(8,128)S(1)}, u32[]{:S(2)}, u32[]{:S(2)}) %collective-permute-start.22) | collective-permute-done | bytes 524320 | tf_op jit(solution)/shard_map/ppermute | solution.py:43
  137.4 0.8 fusion.104
  (99 shorter events, 15.0 us)
Async XLA Ops:
  0.0 34.4 %collective-permute-start = (f32[1,8,32,256]{3,2,1,0:T(8,128)}, f32[1,8,32,256]{3,2,1,0:T(8,128)S(1)}, u32[]{:S(2)}, u32[]{:S(2)}) collective-permute-start(f32[1,8,32,256]{3,2,1,0:T(8,128)} %param.6), channel_id=1, source_target_pairs={{0,8},{8,16},{16,24},{1,9},{9,17},{17,25},{2,10},{10,18},{18,26},{... | collective-permute-start | bytes 786440 | tf_op jit(solution)/shard_map/ppermute | solution.py:21
  5.7 28.7 %collective-permute-start.1 = (f32[1,32,256]{2,1,0:T(8,128)S(1)}, f32[1,32,256]{2,1,0:T(8,128)S(1)}, u32[]{:S(2)}, u32[]{:S(2)}) collective-permute-start(f32[1,32,256]{2,1,0:T(8,128)S(1)} %get-tuple-element.209), channel_id=1, source_target_pairs={{1,0},{2,1},{3,2},{4,3},{5,4},{6,5},{7,6},{0,7},{9,8},{10,9},{11,1... | collective-permute-start | bytes 98312 | tf_op jit(solution)/shard_map/ppermute | solution.py:33
  8.4 26.0 %collective-permute-start.2 = (f32[1,32,256]{2,1,0:T(8,128)S(1)}, f32[1,32,256]{2,1,0:T(8,128)S(1)}, u32[]{:S(2)}, u32[]{:S(2)}) collective-permute-start(f32[1,32,256]{2,1,0:T(8,128)S(1)} %get-tuple-element.210), channel_id=1, source_target_pairs={{0,1},{1,2},{2,3},{3,4},{4,5},{5,6},{6,7},{7,0},{8,9},{9,10},{10,1... | collective-permute-start | bytes 98312 | tf_op jit(solution)/shard_map/ppermute | solution.py:31
  8.4 1.2 copy-start
  9.7 1.0 copy-start.1
  9.7 0.9 copy-start.3
  34.2 1.0 copy-start.2
  35.5 7.3 %collective-permute-start.3 = (f32[8,32,256]{2,1,0:T(8,128)S(1)}, f32[8,32,256]{2,1,0:T(8,128)S(1)}, u32[]{:S(2)}, u32[]{:S(2)}) collective-permute-start(f32[8,32,256]{2,1,0:T(8,128)S(1)} %fusion.92), channel_id=1, source_target_pairs={{0,16},{8,24},{16,0},{24,8},{1,17},{9,25},{17,1},{25,9},{2,18},{10... | collective-permute-start | bytes 786440 | tf_op jit(solution)/shard_map/ppermute | solution.py:43
  42.8 12.0 %collective-permute-start.4 = (f32[2,8,32,256]{3,2,1,0:T(8,128)S(1)}, f32[2,8,32,256]{3,2,1,0:T(8,128)S(1)}, u32[]{:S(2)}, u32[]{:S(2)}) collective-permute-start(f32[2,8,32,256]{3,2,1,0:T(8,128)S(1)} %pad_maximum_fusion.40), channel_id=1, source_target_pairs={{0,8},{8,0},{16,24},{24,16},{1,9},{9,1},{17,25},{25,17},{2,10},{10... | collective-permute-start | bytes 1572872 | tf_op jit(solution)/shard_map/ppermute | solution.py:43
  55.6 5.9 %collective-permute-start.5 = (f32[2,1,32,256]{3,2,1,0:T(8,128)S(1)}, f32[2,1,32,256]{3,2,1,0:T(8,128)S(1)}, u32[]{:S(2)}, u32[]{:S(2)}) collective-permute-start(f32[2,1,32,256]{3,2,1,0:T(8,128)S(1)} %get-tuple-element.195), channel_id=1, source_target_pairs={{1,0},{2,1},{3,2},{4,3},{5,4},{6,5},{7,6},{0,7},{9,8},{10,9},{11,1... | collective-permute-start | bytes 196616 | tf_op jit(solution)/shard_map/ppermute | solution.py:33
  59.7 5.5 %collective-permute-start.6 = (f32[2,1,32,256]{3,2,1,0:T(8,128)S(1)}, f32[2,1,32,256]{3,2,1,0:T(8,128)S(1)}, u32[]{:S(2)}, u32[]{:S(2)}) collective-permute-start(f32[2,1,32,256]{3,2,1,0:T(8,128)S(1)} %get-tuple-element.196), channel_id=1, source_target_pairs={{0,1},{1,2},{2,3},{3,4},{4,5},{5,6},{6,7},{7,0},{8,9},{9,10},{10,1... | collective-permute-start | bytes 196616 | tf_op jit(solution)/shard_map/ppermute | solution.py:31
  66.3 2.4 %collective-permute-start.7 = (f32[2,1,32,256]{3,2,1,0:T(8,128)S(1)}, f32[2,1,32,256]{3,2,1,0:T(8,128)S(1)}, u32[]{:S(2)}, u32[]{:S(2)}) collective-permute-start(f32[2,1,32,256]{3,2,1,0:T(8,128)S(1)} %get-tuple-element.187), channel_id=1, source_target_pairs={{1,0},{2,1},{3,2},{4,3},{5,4},{6,5},{7,6},{0,7},{9,8},{10,9},{11,1... | collective-permute-start | bytes 196616 | tf_op jit(solution)/shard_map/ppermute | solution.py:33
  66.4 5.5 %collective-permute-start.8 = (f32[2,1,32,256]{3,2,1,0:T(8,128)S(1)}, f32[2,1,32,256]{3,2,1,0:T(8,128)S(1)}, u32[]{:S(2)}, u32[]{:S(2)}) collective-permute-start(f32[2,1,32,256]{3,2,1,0:T(8,128)S(1)} %get-tuple-element.188), channel_id=1, source_target_pairs={{0,1},{1,2},{2,3},{3,4},{4,5},{5,6},{6,7},{7,0},{8,9},{9,10},{10,1... | collective-permute-start | bytes 196616 | tf_op jit(solution)/shard_map/ppermute | solution.py:31
  73.1 5.6 %collective-permute-start.10 = (f32[2,1,32,256]{3,2,1,0:T(8,128)S(1)}, f32[2,1,32,256]{3,2,1,0:T(8,128)S(1)}, u32[]{:S(2)}, u32[]{:S(2)}) collective-permute-start(f32[2,1,32,256]{3,2,1,0:T(8,128)S(1)} %get-tuple-element.180), channel_id=1, source_target_pairs={{0,1},{1,2},{2,3},{3,4},{4,5},{5,6},{6,7},{7,0},{8,9},{9,10},{10,1... | collective-permute-start | bytes 196616 | tf_op jit(solution)/shard_map/ppermute | solution.py:31
  73.2 5.5 %collective-permute-start.9 = (f32[2,1,32,256]{3,2,1,0:T(8,128)S(1)}, f32[2,1,32,256]{3,2,1,0:T(8,128)S(1)}, u32[]{:S(2)}, u32[]{:S(2)}) collective-permute-start(f32[2,1,32,256]{3,2,1,0:T(8,128)S(1)} %get-tuple-element.179), channel_id=1, source_target_pairs={{1,0},{2,1},{3,2},{4,3},{5,4},{6,5},{7,6},{0,7},{9,8},{10,9},{11,1... | collective-permute-start | bytes 196616 | tf_op jit(solution)/shard_map/ppermute | solution.py:33
  79.9 5.5 %collective-permute-start.11 = (f32[2,1,32,256]{3,2,1,0:T(8,128)S(1)}, f32[2,1,32,256]{3,2,1,0:T(8,128)S(1)}, u32[]{:S(2)}, u32[]{:S(2)}) collective-permute-start(f32[2,1,32,256]{3,2,1,0:T(8,128)S(1)} %get-tuple-element.171), channel_id=1, source_target_pairs={{1,0},{2,1},{3,2},{4,3},{5,4},{6,5},{7,6},{0,7},{9,8},{10,9},{11,1... | collective-permute-start | bytes 196616 | tf_op jit(solution)/shard_map/ppermute | solution.py:33
  83.5 5.5 %collective-permute-start.12 = (f32[2,1,32,256]{3,2,1,0:T(8,128)S(1)}, f32[2,1,32,256]{3,2,1,0:T(8,128)S(1)}, u32[]{:S(2)}, u32[]{:S(2)}) collective-permute-start(f32[2,1,32,256]{3,2,1,0:T(8,128)S(1)} %get-tuple-element.172), channel_id=1, source_target_pairs={{0,1},{1,2},{2,3},{3,4},{4,5},{5,6},{6,7},{7,0},{8,9},{9,10},{10,1... | collective-permute-start | bytes 196616 | tf_op jit(solution)/shard_map/ppermute | solution.py:31
  90.2 2.4 %collective-permute-start.13 = (f32[2,1,32,256]{3,2,1,0:T(8,128)S(1)}, f32[2,1,32,256]{3,2,1,0:T(8,128)S(1)}, u32[]{:S(2)}, u32[]{:S(2)}) collective-permute-start(f32[2,1,32,256]{3,2,1,0:T(8,128)S(1)} %get-tuple-element.163), channel_id=1, source_target_pairs={{1,0},{2,1},{3,2},{4,3},{5,4},{6,5},{7,6},{0,7},{9,8},{10,9},{11,1... | collective-permute-start | bytes 196616 | tf_op jit(solution)/shard_map/ppermute | solution.py:33
  90.3 5.5 %collective-permute-start.14 = (f32[2,1,32,256]{3,2,1,0:T(8,128)S(1)}, f32[2,1,32,256]{3,2,1,0:T(8,128)S(1)}, u32[]{:S(2)}, u32[]{:S(2)}) collective-permute-start(f32[2,1,32,256]{3,2,1,0:T(8,128)S(1)} %get-tuple-element.164), channel_id=1, source_target_pairs={{0,1},{1,2},{2,3},{3,4},{4,5},{5,6},{6,7},{7,0},{8,9},{9,10},{10,1... | collective-permute-start | bytes 196616 | tf_op jit(solution)/shard_map/ppermute | solution.py:31
  97.0 2.5 %collective-permute-start.15 = (f32[2,1,32,256]{3,2,1,0:T(8,128)S(1)}, f32[2,1,32,256]{3,2,1,0:T(8,128)S(1)}, u32[]{:S(2)}, u32[]{:S(2)}) collective-permute-start(f32[2,1,32,256]{3,2,1,0:T(8,128)S(1)} %get-tuple-element.155), channel_id=1, source_target_pairs={{1,0},{2,1},{3,2},{4,3},{5,4},{6,5},{7,6},{0,7},{9,8},{10,9},{11,1... | collective-permute-start | bytes 196616 | tf_op jit(solution)/shard_map/ppermute | solution.py:33
  97.6 5.6 %collective-permute-start.16 = (f32[2,1,32,256]{3,2,1,0:T(8,128)S(1)}, f32[2,1,32,256]{3,2,1,0:T(8,128)S(1)}, u32[]{:S(2)}, u32[]{:S(2)}) collective-permute-start(f32[2,1,32,256]{3,2,1,0:T(8,128)S(1)} %get-tuple-element.156), channel_id=1, source_target_pairs={{0,1},{1,2},{2,3},{3,4},{4,5},{5,6},{6,7},{7,0},{8,9},{9,10},{10,1... | collective-permute-start | bytes 196616 | tf_op jit(solution)/shard_map/ppermute | solution.py:31
  104.4 2.4 %collective-permute-start.17 = (f32[2,1,32,256]{3,2,1,0:T(8,128)S(1)}, f32[2,1,32,256]{3,2,1,0:T(8,128)S(1)}, u32[]{:S(2)}, u32[]{:S(2)}) collective-permute-start(f32[2,1,32,256]{3,2,1,0:T(8,128)S(1)} %get-tuple-element.147), channel_id=1, source_target_pairs={{1,0},{2,1},{3,2},{4,3},{5,4},{6,5},{7,6},{0,7},{9,8},{10,9},{11,1... | collective-permute-start | bytes 196616 | tf_op jit(solution)/shard_map/ppermute | solution.py:33
  104.5 5.6 %collective-permute-start.18 = (f32[2,1,32,256]{3,2,1,0:T(8,128)S(1)}, f32[2,1,32,256]{3,2,1,0:T(8,128)S(1)}, u32[]{:S(2)}, u32[]{:S(2)}) collective-permute-start(f32[2,1,32,256]{3,2,1,0:T(8,128)S(1)} %get-tuple-element.148), channel_id=1, source_target_pairs={{0,1},{1,2},{2,3},{3,4},{4,5},{5,6},{6,7},{7,0},{8,9},{9,10},{10,1... | collective-permute-start | bytes 196616 | tf_op jit(solution)/shard_map/ppermute | solution.py:31
  111.3 2.5 %collective-permute-start.19 = (f32[2,1,32,256]{3,2,1,0:T(8,128)S(1)}, f32[2,1,32,256]{3,2,1,0:T(8,128)S(1)}, u32[]{:S(2)}, u32[]{:S(2)}) collective-permute-start(f32[2,1,32,256]{3,2,1,0:T(8,128)S(1)} %get-tuple-element.139), channel_id=1, source_target_pairs={{1,0},{2,1},{3,2},{4,3},{5,4},{6,5},{7,6},{0,7},{9,8},{10,9},{11,1... | collective-permute-start | bytes 196616 | tf_op jit(solution)/shard_map/ppermute | solution.py:33
  111.8 5.5 %collective-permute-start.20 = (f32[2,1,32,256]{3,2,1,0:T(8,128)S(1)}, f32[2,1,32,256]{3,2,1,0:T(8,128)S(1)}, u32[]{:S(2)}, u32[]{:S(2)}) collective-permute-start(f32[2,1,32,256]{3,2,1,0:T(8,128)S(1)} %get-tuple-element.140), channel_id=1, source_target_pairs={{0,1},{1,2},{2,3},{3,4},{4,5},{5,6},{6,7},{7,0},{8,9},{9,10},{10,1... | collective-permute-start | bytes 196616 | tf_op jit(solution)/shard_map/ppermute | solution.py:31
  118.1 9.7 %collective-permute-start.21 = (f32[2,8,32,256]{3,2,1,0:T(8,128)S(1)}, f32[2,8,32,256]{3,2,1,0:T(8,128)S(1)}, u32[]{:S(2)}, u32[]{:S(2)}) collective-permute-start(f32[2,8,32,256]{3,2,1,0:T(8,128)S(1)} %pad_maximum_fusion.41), channel_id=1, source_target_pairs={{0,8},{8,0},{16,24},{24,16},{1,9},{9,1},{17,25},{25,17},{2,10},{10... | collective-permute-start | bytes 1572872 | tf_op jit(solution)/shard_map/ppermute | solution.py:43
  128.1 9.2 %collective-permute-start.22 = (f32[2,8,32,256]{3,2,1,0:T(8,128)S(1)}, f32[2,8,32,256]{3,2,1,0:T(8,128)S(1)}, u32[]{:S(2)}, u32[]{:S(2)}) collective-permute-start(f32[2,8,32,256]{3,2,1,0:T(8,128)S(1)} %fusion.88), channel_id=1, source_target_pairs={{0,16},{8,24},{16,0},{24,8},{1,17},{9,25},{17,1},{25,9},{2,18},{10... | collective-permute-start | bytes 1572872 | tf_op jit(solution)/shard_map/ppermute | solution.py:43
where the time goes:
time: 139 us; the launch traced here: 138 us
  waiting for transfers between devices  70.4 us (51%)
  starting transfers between devices  28 us (20%)
  other arithmetic  23.9 us (17%)
  local copies, waits for them, and re-layouts  14.5 us (10%)
    ppermute x4, waiting for transfers between devices, partner_2(): return lax.ppermute(value, axis, pairs)  31.3 us
    ppermute x9, waiting for transfers between devices, extended(): lax.ppermute(tail, axis, [(i, (i + 1) % count) for i in range(count)])  26.3 us
    ppermute x9, starting transfers between devices, extended(): lax.ppermute(head, axis, [((i + 1) % count, i) for i in range(count)])  15.3 us
    ppermute x9, waiting for transfers between devices, extended(): lax.ppermute(head, axis, [((i + 1) % count, i) for i in range(count)])  12.8 us
    add x16, other arithmetic, add_grain(): summed + jnp.where(labels == grain_id, rate_table[grain_id], jnp.zeros(()...  12.5 us
    dynamic_slice x16, local copies, waits for them, and re-layouts, add_grain(): rate_table[grain_id]  10.7 us
    ppermute x4, starting transfers between devices, partner_2(): return lax.ppermute(value, axis, pairs)  6.27 us
    another operation x51, other arithmetic, complex_times(): jnp.stack([left_val[0] * right_val[0] - left_val[1] * right_val[1], left_...  5.02 us
  transfers between devices with their start and end apart: 23, of which 19 were waited for; matrix products, arithmetic and copies ran while one was open for 19% of the time, Pallas kernels for 0%

commit v1 on v0

--- a/solution.py
+++ b/solution.py
@@ -1,10 +1,14 @@
+import functools
 import math
 
 import jax
 import jax.numpy as jnp
 from jax import lax
+from jax.experimental import pallas as pl
+from jax.experimental.pallas import tpu as pltpu
 from jax.sharding import PartitionSpec as P
 
+MESH = pl.DeviceIdType.MESH
 SWEEPS = 8
 GRAINS = 16
 
@@ -147,7 +151,336 @@
     return state - correction
 
 
+def ring_place(index):
+    return index + index // 2 * (5 - 2 * index)
+
+
+def grain_rates(labels, table_ref):
+    rate = jnp.zeros(labels.shape, jnp.float32)
+    for grain_id in range(GRAINS):
+        rate = jnp.where(labels == grain_id, table_ref[grain_id], rate)
+    return rate
+
+
+def paradiag_kernel(
+    slabs,
+    table_ref,
+    state_ref,
+    initial_ref,
+    labels_ref,
+    out_ref,
+    home,
+    chunk,
+    first,
+    classes,
+    rows_out,
+    rows_in,
+    planes_in,
+    coupling,
+    base,
+    sol,
+    sol_planes,
+    edge_rows,
+    sol_rows,
+    result,
+    local_sem,
+    a2a_send,
+    a2a_recv,
+    rows_send,
+    rows_recv,
+    planes_send,
+    planes_recv,
+    sweep_send,
+    sweep_recv,
+    back_send,
+    back_recv,
+):
+    t = lax.axis_index("tm")
+    s = lax.axis_index("space")
+    p = ring_place(t)
+    below, above = lax.rem(s + slabs - 1, slabs), lax.rem(s + 1, slabs)
+    depth, width = home.shape[0], home.shape[2]
+    my_rows = pl.ds(pl.multiple_of(p * 8, 8), 8)
+
+    barrier = pltpu.get_barrier_semaphore()
+    for ahead in range(1, 4):
+        pl.semaphore_signal(
+            barrier, inc=1, device_id=(lax.rem(t + ahead, 4), s), device_id_type=MESH
+        )
+    for ahead in range(4):
+        for slab in (below, above):
+            pl.semaphore_signal(
+                barrier, inc=1, device_id=(lax.rem(t + ahead, 4), slab), device_id_type=MESH
+            )
+
+    load_home = pltpu.make_async_copy(state_ref.at[0], home, local_sem.at[0])
+    load_home.start()
+    load_classes = pltpu.make_async_copy(labels_ref.at[:, my_rows, :], classes, local_sem.at[1])
+    load_classes.start()
+    load_chunk = pltpu.make_async_copy(
+        state_ref.at[0, :, my_rows, :], chunk.at[t], local_sem.at[2]
+    )
+    load_chunk.start()
+    load_first = pltpu.make_async_copy(initial_ref.at[:, my_rows, :], first, local_sem.at[3])
+    load_first.start()
+
+    load_home.wait()
+    for place in range(4):
+        for side, row in enumerate(((8 * place + 31) % 32, (8 * place + 8) % 32)):
+            for z in range(depth):
+                rows_out[place, side, z : z + 1, :] = home[z, row : row + 1, :]
+    load_rows = pltpu.make_async_copy(rows_out.at[p], rows_in.at[t], local_sem.at[4])
+    load_rows.start()
+
+    pl.semaphore_wait(barrier, 11)
+
+    sends = []
+    for ahead in (2, 1, 3):
+        other = lax.rem(t + ahead, 4)
+        place = ring_place(other)
+        other_rows = pl.ds(pl.multiple_of(place * 8, 8), 8)
+        sends.append(
+            pltpu.make_async_remote_copy(
+                src_ref=home.at[:, other_rows, :],
+                dst_ref=chunk.at[t],
+                send_sem=a2a_send.at[ahead],
+                recv_sem=a2a_recv.at[4 - ahead],
+                device_id=(other, s),
+                device_id_type=MESH,
+            )
+        )
+        sends.append(
+            pltpu.make_async_remote_copy(
+                src_ref=rows_out.at[place],
+                dst_ref=rows_in.at[t],
+                send_sem=rows_send.at[ahead],
+                recv_sem=rows_recv.at[4 - ahead],
+                device_id=(other, s),
+                device_id_type=MESH,
+            )
+        )
+    for ahead in range(4):
+        other = lax.rem(t + ahead, 4)
+        place = ring_place(other)
+        other_rows = pl.ds(pl.multiple_of(place * 8, 8), 8)
+        for side, (slab, plane) in enumerate(((above, depth - 1), (below, 0))):
+            sends.append(
+                pltpu.make_async_remote_copy(
+                    src_ref=home.at[plane, other_rows, :],
+                    dst_ref=planes_in.at[t, side],
+                    send_sem=planes_send.at[ahead, side],
+                    recv_sem=planes_recv.at[(4 - ahead) % 4, side],
+                    device_id=(other, slab),
+                    device_id_type=MESH,
+                )
+            )
+    for copy in sends:
+        copy.start()
+
+    row_number = lax.broadcasted_iota(jnp.int32, (8, width), 0)
+    top, bottom = row_number == 0, row_number == 7
+    beta = alpha_wrap**0.25
+
+    load_classes.wait()
+    for z in range(depth):
+        rate = grain_rates(classes[z], table_ref)
+        real_part = 1.0 + diag_extra * rate
+        scale = 1.0 / (real_part * real_part + beta * beta)
+        coupling[0, z] = 1.0 / (real_part - beta)
+        coupling[1, z] = 1.0 / (real_part + beta)
+        coupling[2, z] = real_part * scale
+        coupling[3, z] = -beta * scale
+        coupling[4, z] = rate
+
+    load_first.wait()
+    load_chunk.wait()
+    load_rows.wait()
+    for copy in sends:
+        copy.wait_recv()
+
+    def plane_neighbours(value, row_before, row_after):
+        summed = jnp.where(top, row_before, pltpu.roll(value, 1, 0))
+        summed += jnp.where(bottom, row_after, pltpu.roll(value, 7, 0))
+        return summed + (pltpu.roll(value, 1, 1) + pltpu.roll(value, width - 1, 1))
+
+    def put_edges(slot, field, z, value):
+        edge_rows[slot, 0, field, z : z + 1, :] = value[7:8, :]
+        edge_rows[slot, 1, field, z : z + 1, :] = value[0:1, :]
+
+    for z in range(depth):
+        rate = coupling[4, z]
+        scaled = []
+        for n in range(4):
+            value = chunk[n, z]
+            around = plane_neighbours(
+                value, rows_in[n, 0, z : z + 1, :], rows_in[n, 1, z : z + 1, :]
+            )
+            around += chunk[n, z - 1] if z > 0 else planes_in[n, 0]
+            around += chunk[n, z + 1] if z < depth - 1 else planes_in[n, 1]
+            earlier = chunk[n - 1, z] if n > 0 else first[z]
+            laplacian = around - 6.0 * value
+            residual = (
+                value
+                - earlier
+                + tau_step * rate * (value * value * value - value - kappa_grad * laplacian)
+            )
+            scaled.append(residual * alpha_wrap ** (n / 4))
+        even, odd = scaled[0] + scaled[2], scaled[1] + scaled[3]
+        rhs_real, rhs_imag = scaled[0] - scaled[2], scaled[3] - scaled[1]
+        inv_real, inv_imag = coupling[2, z], coupling[3, z]
+        starts = (
+            (even + odd) * coupling[0, z],
+            (even - odd) * coupling[1, z],
+            rhs_real * inv_real - rhs_imag * inv_imag,
+            rhs_real * inv_imag + rhs_imag * inv_real,
+        )
+        for field in range(4):
+            base[field, z] = starts[field]
+            sol[0, field, z] = starts[field]
+            put_edges(0, field, z, starts[field])
+            coupling[field, z] = coupling[field, z] * rate
+
+    before, after = ring_place(lax.rem(p + 3, 4)), ring_place(lax.rem(p + 1, 4))
+
+    def sweep_copies(j):
+        copies = []
+        for side, (slab, plane) in enumerate(((above, depth - 1), (below, 0))):
+            copies.append(
+                pltpu.make_async_remote_copy(
+                    src_ref=sol.at[j, :, plane],
+                    dst_ref=sol_planes.at[j, side],
+                    send_sem=sweep_send.at[j, side],
+                    recv_sem=sweep_recv.at[j, side],
+                    device_id=(t, slab),
+                    device_id_type=MESH,
+                )
+            )
+        for side, other in enumerate((after, before)):
+            copies.append(
+                pltpu.make_async_remote_copy(
+                    src_ref=edge_rows.at[j, side],
+                    dst_ref=sol_rows.at[j, side],
+                    send_sem=sweep_send.at[j, 2 + side],
+                    recv_sem=sweep_recv.at[j, 2 + side],
+                    device_id=(other, s),
+                    device_id_type=MESH,
+                )
+            )
+        return copies
+
+    def sweep(j, carry):
+        copies = sweep_copies(j)
+        for copy in copies:
+            copy.start()
+        for copy in copies:
+            copy.wait_recv()
+        for z in range(depth):
+            sums = []
+            for field in range(4):
+                around = plane_neighbours(
+                    sol[j, field, z],
+                    sol_rows[j, 0, field, z : z + 1, :],
+                    sol_rows[j, 1, field, z : z + 1, :],
+                )
+                around += sol[j, field, z - 1] if z > 0 else sol_planes[j, 0, field]
+                around += sol[j, field, z + 1] if z < depth - 1 else sol_planes[j, 1, field]
+                sums.append(around)
+            made = (
+                base[0, z] + coupling[0, z] * sums[0],
+                base[1, z] + coupling[1, z] * sums[1],
+                base[2, z] + coupling[2, z] * sums[2] - coupling[3, z] * sums[3],
+                base[3, z] + coupling[2, z] * sums[3] + coupling[3, z] * sums[2],
+            )
+            for field in range(4):
+                sol[j + 1, field, z] = made[field]
+                put_edges(j + 1, field, z, made[field])
+        return carry
+
+    lax.fori_loop(0, SWEEPS, sweep, 0)
+
+    for z in range(depth):
+        zero, two, real, imag = (sol[SWEEPS, field, z] for field in range(4))
+        plus, minus = zero + two, zero - two
+        back = (plus + 2.0 * real, minus - 2.0 * imag, plus - 2.0 * real, minus + 2.0 * imag)
+        for n in range(4):
+            result[n, z] = chunk[n, z] - back[n] * (0.25 * alpha_wrap ** (-n / 4))
+    returns = []
+    for ahead in (2, 1, 3):
+        other = lax.rem(t + ahead, 4)
+        returns.append(
+            pltpu.make_async_remote_copy(
+                src_ref=result.at[other],
+                dst_ref=out_ref.at[:, my_rows, :],
+                send_sem=back_send.at[ahead],
+                recv_sem=back_recv.at[4 - ahead],
+                device_id=(other, s),
+                device_id_type=MESH,
+            )
+        )
+    for copy in returns:
+        copy.start()
+    keep = pltpu.make_async_copy(result.at[t], out_ref.at[:, my_rows, :], local_sem.at[5])
+    keep.start()
+    for copy in sends:
+        copy.wait_send()
+
+    def drain(j, carry):
+        for copy in sweep_copies(j):
+            copy.wait_send()
+        return carry
+
+    lax.fori_loop(0, SWEEPS, drain, 0)
+    keep.wait()
+    for copy in returns:
+        copy.wait()
+
+
+def fused_shards(state, initial, labels, mobility_table):
+    _, depth, rows, width = state.shape
+    slabs = lax.axis_size("space")
+    f32 = jnp.float32
+    dma = pltpu.SemaphoreType.DMA
+    new_state = pl.pallas_call(
+        functools.partial(paradiag_kernel, slabs),
+        out_shape=jax.ShapeDtypeStruct((depth, rows, width), f32),
+        in_specs=[pl.BlockSpec(memory_space=pltpu.SMEM)] + [pl.BlockSpec(memory_space=pl.ANY)] * 3,
+        out_specs=pl.BlockSpec(memory_space=pltpu.VMEM),
+        scratch_shapes=[
+            pltpu.VMEM((depth, rows, width), f32),
+            pltpu.VMEM((4, depth, 8, width), f32),
+            pltpu.VMEM((depth, 8, width), f32),
+            pltpu.VMEM((depth, 8, width), jnp.int32),
+            pltpu.VMEM((4, 2, depth, width), f32),
+            pltpu.VMEM((4, 2, depth, width), f32),
+            pltpu.VMEM((4, 2, 8, width), f32),
+            pltpu.VMEM((5, depth, 8, width), f32),
+            pltpu.VMEM((4, depth, 8, width), f32),
+            pltpu.VMEM((SWEEPS + 1, 4, depth, 8, width), f32),
+            pltpu.VMEM((SWEEPS, 2, 4, 8, width), f32),
+            pltpu.VMEM((SWEEPS + 1, 2, 4, depth, width), f32),
+            pltpu.VMEM((SWEEPS, 2, 4, depth, width), f32),
+            pltpu.VMEM((4, depth, 8, width), f32),
+            dma((6,)),
+            dma((4,)),
+            dma((4,)),
+            dma((4,)),
+            dma((4,)),
+            dma((4, 2)),
+            dma((4, 2)),
+            dma((SWEEPS, 4)),
+            dma((SWEEPS, 4)),
+            dma((4,)),
+            dma((4,)),
+        ],
+        compiler_params=pltpu.CompilerParams(
+            collective_id=0, has_side_effects=True, vmem_limit_bytes=24 * 2**20
+        ),
+    )(mobility_table, state, initial, labels)
+    return new_state[None]
+
+
 def solution(mesh):
     in_specs = (P("tm", "space", None, None), P("space", None, None), P("space", None, None), P())
     out_specs = P("tm", "space", None, None)
-    return jax.shard_map(shards, mesh=mesh, in_specs=in_specs, out_specs=out_specs, check_vma=False)
+    body = fused_shards if mesh.shape["tm"] == 4 and mesh.shape["space"] > 2 else shards
+    return jax.shard_map(body, mesh=mesh, in_specs=in_specs, out_specs=out_specs, check_vma=False)

time: 139 us -> 50.8 us (0.37)
  waiting for transfers between devices: 70.4 us -> 0 us
  Pallas kernels: 0 us -> 46.4 us
  starting transfers between devices: 28 us -> 0 us
  other arithmetic: 23.9 us -> 0 us
  local copies, waits for them, and re-layouts: 14.5 us -> 4.21 us
    ppermute x23 -> x0, waiting for transfers between devices: 70.4 us -> none  [the longest x4 31.3 us: partner_2(): return lax.ppermute(value, axis, pairs)]
    pallas_call x0 -> x1, Pallas kernels: none -> 46.4 us  [fused_shards(): pl.pallas_call(functools.partial(paradiag_kernel, slabs), out_shape=jax.S...]
    ppermute x23 -> x0, starting transfers between devices: 28 us -> none  [the longest x9 15.3 us: extended(): lax.ppermute(head, axis, [((i + 1) % count, i) for i in range(count)])]
    add x24 -> x0, other arithmetic: 17.1 us -> none  [the longest x16 12.5 us: add_grain(): summed + jnp.where(labels == grain_id, rate_table[grain_id], jnp.zeros(()...]
    dynamic_slice x16 -> x0, local copies, waits for them, and re-layouts: 10.7 us -> none  [add_grain(): rate_table[grain_id]]
    another operation x53 -> x0, other arithmetic: 5.12 us -> none  [the longest x51 5.02 us: complex_times(): jnp.stack([left_val[0] * right_val[0] - left_val[1] * right_val[1], left_...]
    unnamed x8 -> x9, local copies, waits for them, and re-layouts: 1.64 us -> 4.21 us
    slice x5 -> x0, local copies, waits for them, and re-layouts: 2.17 us -> none  [the longest x2 1.32 us: plane_sum(): return summed + jnp.roll(grid_field, 1, -1) + jnp.roll(grid_field, -1, -1)]
  transfers between devices with their start and end apart: 23 -> 0, of which waited for: 19 -> 0; matrix products, arithmetic and copies ran while one was open for 19% -> 0% of each run, Pallas kernels for 0% -> 0%
where the time goes in v1:
time: 50.8 us; the launch traced here: 50.6 us
  Pallas kernels  46.4 us (91%)
  local copies, waits for them, and re-layouts  4.21 us (8%)
    pallas_call x1, Pallas kernels, fused_shards(): pl.pallas_call(functools.partial(paradiag_kernel, slabs), out_shape=jax.S...  46.4 us
    unnamed x9, local copies, waits for them, and re-layouts  4.21 us

profile of v1, /device:TPU:0, one launch (start us, length us, event | category | flops | bytes accessed | tf_op | source)
XLA Modules:
  0.0 50.6 jit_solution(5481942628952201743)
XLA Ops:
  0.0 0.0 copy-start
  0.0 0.9 %copy-done = f32[1,8,32,256]{3,2,1,0:T(8,128)S(1)} copy-done((f32[1,8,32,256]{3,2,1,0:T(8,128)S(1)}, f32[1,8,32,256]{3,2,1,0:T(8,128)}, u32[]{:S(2)}) %copy-start) | copy-done | bytes 262168
  1.0 0.0 copy-start.1
  1.0 0.9 %copy-done.1 = f32[8,32,256]{2,1,0:T(8,128)S(1)} copy-done((f32[8,32,256]{2,1,0:T(8,128)S(1)}, f32[8,32,256]{2,1,0:T(8,128)}, u32[]{:S(2)}) %copy-start.1) | copy-done | bytes 262168
  1.9 0.0 copy-start.2
  1.9 0.9 %copy-done.2 = s32[8,32,256]{2,1,0:T(8,128)S(1)} copy-done((s32[8,32,256]{2,1,0:T(8,128)S(1)}, s32[8,32,256]{2,1,0:T(8,128)}, u32[]{:S(2)}) %copy-start.2) | copy-done | bytes 262168
  2.9 0.0 copy-start.3
  2.9 0.7 %copy-done.3 = f32[16]{0:T(128)S(1)} copy-done((f32[16]{0:T(128)S(1)}, f32[16]{0:T(128)}, u32[]{:S(2)}) %copy-start.3) | copy-done | bytes 88
  3.5 46.4 %shard_map.46 = f32[8,32,256]{2,1,0:T(8,128)S(1)} custom-call(f32[16]{0:T(128)S(1)} %copy-done.3, f32[1,8,32,256]{3,2,1,0:T(8,128)S(1)} %copy-done, f32[8,32,256]{2,1,0:T(8,128)S(1)} %copy-done.1, s32[8,32,256]{2,1,0:T(8,128)S(1)} %copy-done.2), custom_call_target="tpu_custom_call" | custom-call | tf_op jit(solution)/shard_map/pallas_call | solution.py:443
  49.9 0.7 %copy.6 = f32[1,8,32,256]{3,2,1,0:T(8,128)} copy(f32[1,8,32,256]{3,2,1,0:T(8,128)S(1)} %bitcast.1) | data formatting | bytes 524288
Async XLA Ops:
  0.0 0.9 %copy-start = (f32[1,8,32,256]{3,2,1,0:T(8,128)S(1)}, f32[1,8,32,256]{3,2,1,0:T(8,128)}, u32[]{:S(2)}) copy-start(f32[1,8,32,256]{3,2,1,0:T(8,128)} %state_ref.1) | copy-start | bytes 786436
  1.0 0.9 %copy-start.1 = (f32[8,32,256]{2,1,0:T(8,128)S(1)}, f32[8,32,256]{2,1,0:T(8,128)}, u32[]{:S(2)}) copy-start(f32[8,32,256]{2,1,0:T(8,128)} %initial_ref.1) | copy-start | bytes 786436
  1.9 0.9 %copy-start.2 = (s32[8,32,256]{2,1,0:T(8,128)S(1)}, s32[8,32,256]{2,1,0:T(8,128)}, u32[]{:S(2)}) copy-start(s32[8,32,256]{2,1,0:T(8,128)} %labels_ref.1) | copy-start | bytes 786436
  2.9 0.7 %copy-start.3 = (f32[16]{0:T(128)S(1)}, f32[16]{0:T(128)}, u32[]{:S(2)}) copy-start(f32[16]{0:T(128)} %table_ref.1) | copy-start | bytes 196

commit v2 on v1

--- a/solution.py
+++ b/solution.py
@@ -10,6 +10,8 @@
 
 MESH = pl.DeviceIdType.MESH
 SWEEPS = 8
+HALO = 4
+BLOCKS = SWEEPS // HALO
 GRAINS = 16
 
 
@@ -177,11 +179,13 @@
     rows_in,
     planes_in,
     coupling,
+    box_coupling,
     base,
     sol,
-    sol_planes,
-    edge_rows,
-    sol_rows,
+    own,
+    own_in,
+    edges,
+    edges_in,
     result,
     local_sem,
     a2a_send,
@@ -190,8 +194,10 @@
     rows_recv,
     planes_send,
     planes_recv,
-    sweep_send,
-    sweep_recv,
+    class_send,
+    class_recv,
+    halo_send,
+    halo_recv,
     back_send,
     back_recv,
 ):
@@ -215,8 +221,19 @@
 
     load_home = pltpu.make_async_copy(state_ref.at[0], home, local_sem.at[0])
     load_home.start()
-    load_classes = pltpu.make_async_copy(labels_ref.at[:, my_rows, :], classes, local_sem.at[1])
-    load_classes.start()
+    chunk_rows = [
+        pl.ds(pl.multiple_of(lax.rem(p + shift, 4) * 8, 8), 8) for shift in (3, 0, 1)
+    ]
+    load_classes = [
+        pltpu.make_async_copy(
+            labels_ref.at[:, chunk_rows[side], :],
+            classes.at[pl.ds(HALO, depth), side],
+            local_sem.at[6 + side],
+        )
+        for side in range(3)
+    ]
+    for copy in load_classes:
+        copy.start()
     load_chunk = pltpu.make_async_copy(
         state_ref.at[0, :, my_rows, :], chunk.at[t], local_sem.at[2]
     )
@@ -274,16 +291,33 @@
                     device_id_type=MESH,
                 )
             )
-    for copy in sends:
+    class_sends = []
+    for side in range(3):
+        for way, (slab, start, place) in enumerate(
+            ((above, depth - HALO, 0), (below, 0, HALO + depth))
+        ):
+            class_sends.append(
+                pltpu.make_async_remote_copy(
+                    src_ref=labels_ref.at[pl.ds(start, HALO), chunk_rows[side], :],
+                    dst_ref=classes.at[pl.ds(place, HALO), side],
+                    send_sem=class_send.at[side, way],
+                    recv_sem=class_recv.at[side, way],
+                    device_id=(t, slab),
+                    device_id_type=MESH,
+                )
+            )
+    for copy in sends + class_sends:
         copy.start()
 
     row_number = lax.broadcasted_iota(jnp.int32, (8, width), 0)
     top, bottom = row_number == 0, row_number == 7
+    upper = row_number < 4
     beta = alpha_wrap**0.25
 
-    load_classes.wait()
+    for copy in load_classes:
+        copy.wait()
     for z in range(depth):
-        rate = grain_rates(classes[z], table_ref)
+        rate = grain_rates(classes[HALO + z, 1], table_ref)
         real_part = 1.0 + diag_extra * rate
         scale = 1.0 / (real_part * real_part + beta * beta)
         coupling[0, z] = 1.0 / (real_part - beta)
@@ -292,6 +326,32 @@
         coupling[3, z] = -beta * scale
         coupling[4, z] = rate
 
+    for copy in class_sends:
+        copy.wait_recv()
+
+    def swap(value):
+        return pltpu.roll(value, 4, 0)
+
+    def box_plane(z, carry):
+        middle = swap(classes[z, 1])
+        for part, label in enumerate(
+            (
+                jnp.where(upper, swap(classes[z, 0]), middle),
+                jnp.where(upper, middle, swap(classes[z, 2])),
+            )
+        ):
+            rate = grain_rates(label, table_ref)
+            real_part = 1.0 + diag_extra * rate
+            scale = rate / (real_part * real_part + beta * beta)
+            rows = slice(8 * part, 8 * part + 8)
+            box_coupling[0, z, rows] = rate / (real_part - beta)
+            box_coupling[1, z, rows] = rate / (real_part + beta)
+            box_coupling[2, z, rows] = real_part * scale
+            box_coupling[3, z, rows] = beta * scale
+        return carry
+
+    lax.fori_loop(0, depth + 2 * HALO, box_plane, 0)
+
     load_first.wait()
     load_chunk.wait()
     load_rows.wait()
@@ -302,10 +362,6 @@
         summed = jnp.where(top, row_before, pltpu.roll(value, 1, 0))
         summed += jnp.where(bottom, row_after, pltpu.roll(value, 7, 0))
         return summed + (pltpu.roll(value, 1, 1) + pltpu.roll(value, width - 1, 1))
-
-    def put_edges(slot, field, z, value):
-        edge_rows[slot, 0, field, z : z + 1, :] = value[7:8, :]
-        edge_rows[slot, 1, field, z : z + 1, :] = value[0:1, :]
 
     for z in range(depth):
         rate = coupling[4, z]
@@ -335,71 +391,121 @@
             rhs_real * inv_imag + rhs_imag * inv_real,
         )
         for field in range(4):
-            base[field, z] = starts[field]
-            sol[0, field, z] = starts[field]
-            put_edges(0, field, z, starts[field])
-            coupling[field, z] = coupling[field, z] * rate
+            own[0, field, z] = starts[field]
 
     before, after = ring_place(lax.rem(p + 3, 4)), ring_place(lax.rem(p + 1, 4))
 
-    def sweep_copies(j):
-        copies = []
-        for side, (slab, plane) in enumerate(((above, depth - 1), (below, 0))):
-            copies.append(
-                pltpu.make_async_remote_copy(
-                    src_ref=sol.at[j, :, plane],
-                    dst_ref=sol_planes.at[j, side],
-                    send_sem=sweep_send.at[j, side],
-                    recv_sem=sweep_recv.at[j, side],
-                    device_id=(t, slab),
-                    device_id_type=MESH,
+    def block_copies(block):
+        moves = []
+        for side, (slab, start) in enumerate(((above, depth - HALO), (below, 0))):
+            moves.append(
+                (own.at[block, :, pl.ds(start, HALO)], own_in.at[block, side], (t, slab))
+            )
+        for side, other in enumerate((after, before)):
+            moves.append(
+                (edges.at[block, side], edges_in.at[block, side, pl.ds(1, 2)], (other, s))
+            )
+            for slab, half, place in ((above, 1, 0), (below, 0, 3)):
+                moves.append(
+                    (
+                        edges.at[block, side, half],
+                        edges_in.at[block, side, place],
+                        (other, slab),
+                    )
                 )
-            )
-        for side, other in enumerate((after, before)):
-            copies.append(
-                pltpu.make_async_remote_copy(
-                    src_ref=edge_rows.at[j, side],
-                    dst_ref=sol_rows.at[j, side],
-                    send_sem=sweep_send.at[j, 2 + side],
-                    recv_sem=sweep_recv.at[j, 2 + side],
-                    device_id=(other, s),
-                    device_id_type=MESH,
-                )
-            )
-        return copies
-
-    def sweep(j, carry):
-        copies = sweep_copies(j)
+        return [
+            pltpu.make_async_remote_copy(
+                src_ref=source,
+                dst_ref=target,
+                send_sem=halo_send.at[block, number],
+                recv_sem=halo_recv.at[block, number],
+                device_id=device,
+                device_id_type=MESH,
+            )
+            for number, (source, target, device) in enumerate(moves)
+        ]
+
+    def put_edges(block):
+        def of_field(field, carry):
+            for half in range(2):
+                for i in range(2):
+                    one = own[block, field, 4 * half + i]
+                    two = own[block, field, 4 * half + i + 2]
+                    edges[block, 0, half, field, i] = jnp.where(upper, swap(one), two)
+                    edges[block, 1, half, field, i] = jnp.where(upper, one, swap(two))
+            return carry
+
+        lax.fori_loop(0, 4, of_field, 0)
+
+    def assemble(block, target):
+        def of_field(field, carry):
+            for z in range(depth + 2 * HALO):
+                quarter, late, i = z // 4, z % 4 // 2, z % 2
+                if quarter == 0:
+                    middle = own_in[block, 0, field, z]
+                elif quarter == 3:
+                    middle = own_in[block, 1, field, z - HALO - depth]
+                else:
+                    middle = own[block, field, z - HALO]
+                middle = swap(middle)
+                low = edges_in[block, 0, quarter, field, i]
+                high = edges_in[block, 1, quarter, field, i]
+                low = swap(low) if late else low
+                high = high if late else swap(high)
+                target[field, z, 0:8] = jnp.where(upper, low, middle)
+                target[field, z, 8:16] = jnp.where(upper, middle, high)
+            return carry
+
+        lax.fori_loop(0, 4, of_field, 0)
+
+    def sweep(source, target, first_plane, last_plane):
+        def two_planes(pair, carry):
+            for extra in range(2):
+                z = first_plane + 2 * pair + extra
+                sums = []
+                for field in range(4):
+                    value = source[field, z]
+                    around = pltpu.roll(value, 1, 0) + pltpu.roll(value, 15, 0)
+                    around += pltpu.roll(value, 1, 1) + pltpu.roll(value, width - 1, 1)
+                    sums.append(around + (source[field, z - 1] + source[field, z + 1]))
+                real, imag = box_coupling[2, z], box_coupling[3, z]
+                target[0, z] = base[0, z] + box_coupling[0, z] * sums[0]
+                target[1, z] = base[1, z] + box_coupling[1, z] * sums[1]
+                target[2, z] = base[2, z] + real * sums[2] + imag * sums[3]
+                target[3, z] = base[3, z] + real * sums[3] - imag * sums[2]
+            return carry
+
+        lax.fori_loop(0, (last_plane - first_plane) // 2, two_planes, 0)
+
+    halos = []
+    for block in range(BLOCKS):
+        put_edges(block)
+        copies = block_copies(block)
+        halos += copies
         for copy in copies:
             copy.start()
         for copy in copies:
             copy.wait_recv()
-        for z in range(depth):
-            sums = []
-            for field in range(4):
-                around = plane_neighbours(
-                    sol[j, field, z],
-                    sol_rows[j, 0, field, z : z + 1, :],
-                    sol_rows[j, 1, field, z : z + 1, :],
+        source = base if block == 0 else sol.at[0]
+        assemble(block, source)
+        for step in range(HALO):
+            target = sol.at[(step + 1) % 2]
+            sweep(source, target, step + 1, depth + 2 * HALO - 1 - step)
+            source = target
+
+        def take_own(field, carry):
+            for z in range(depth):
+                own[block + 1, field, z] = jnp.where(
+                    upper,
+                    swap(sol[0, field, HALO + z, 0:8]),
+                    swap(sol[0, field, HALO + z, 8:16]),
                 )
-                around += sol[j, field, z - 1] if z > 0 else sol_planes[j, 0, field]
-                around += sol[j, field, z + 1] if z < depth - 1 else sol_planes[j, 1, field]
-                sums.append(around)
-            made = (
-                base[0, z] + coupling[0, z] * sums[0],
-                base[1, z] + coupling[1, z] * sums[1],
-                base[2, z] + coupling[2, z] * sums[2] - coupling[3, z] * sums[3],
-                base[3, z] + coupling[2, z] * sums[3] + coupling[3, z] * sums[2],
-            )
-            for field in range(4):
-                sol[j + 1, field, z] = made[field]
-                put_edges(j + 1, field, z, made[field])
-        return carry
-
-    lax.fori_loop(0, SWEEPS, sweep, 0)
+            return carry
+
+        lax.fori_loop(0, 4, take_own, 0)
 
     for z in range(depth):
-        zero, two, real, imag = (sol[SWEEPS, field, z] for field in range(4))
+        zero, two, real, imag = (own[BLOCKS, field, z] for field in range(4))
         plus, minus = zero + two, zero - two
         back = (plus + 2.0 * real, minus - 2.0 * imag, plus - 2.0 * real, minus + 2.0 * imag)
         for n in range(4):
@@ -421,15 +527,8 @@
         copy.start()
     keep = pltpu.make_async_copy(result.at[t], out_ref.at[:, my_rows, :], local_sem.at[5])
     keep.start()
-    for copy in sends:
+    for copy in sends + class_sends + halos:
         copy.wait_send()
-
-    def drain(j, carry):
-        for copy in sweep_copies(j):
-            copy.wait_send()
-        return carry
-
-    lax.fori_loop(0, SWEEPS, drain, 0)
     keep.wait()
     for copy in returns:
         copy.wait()
@@ -449,31 +548,35 @@
             pltpu.VMEM((depth, rows, width), f32),
             pltpu.VMEM((4, depth, 8, width), f32),
             pltpu.VMEM((depth, 8, width), f32),
-            pltpu.VMEM((depth, 8, width), jnp.int32),
+            pltpu.VMEM((depth + 2 * HALO, 3, 8, width), jnp.int32),
             pltpu.VMEM((4, 2, depth, width), f32),
             pltpu.VMEM((4, 2, depth, width), f32),
             pltpu.VMEM((4, 2, 8, width), f32),
             pltpu.VMEM((5, depth, 8, width), f32),
+            pltpu.VMEM((4, depth + 2 * HALO, 16, width), f32),
+            pltpu.VMEM((4, depth + 2 * HALO, 16, width), f32),
+            pltpu.VMEM((2, 4, depth + 2 * HALO, 16, width), f32),
+            pltpu.VMEM((BLOCKS + 1, 4, depth, 8, width), f32),
+            pltpu.VMEM((BLOCKS, 2, 4, HALO, 8, width), f32),
+            pltpu.VMEM((BLOCKS, 2, 2, 4, 2, 8, width), f32),
+            pltpu.VMEM((BLOCKS, 2, 4, 4, 2, 8, width), f32),
             pltpu.VMEM((4, depth, 8, width), f32),
-            pltpu.VMEM((SWEEPS + 1, 4, depth, 8, width), f32),
-            pltpu.VMEM((SWEEPS, 2, 4, 8, width), f32),
-            pltpu.VMEM((SWEEPS + 1, 2, 4, depth, width), f32),
-            pltpu.VMEM((SWEEPS, 2, 4, depth, width), f32),
-            pltpu.VMEM((4, depth, 8, width), f32),
-            dma((6,)),
+            dma((9,)),
             dma((4,)),
             dma((4,)),
             dma((4,)),
             dma((4,)),
             dma((4, 2)),
             dma((4, 2)),
-            dma((SWEEPS, 4)),
-            dma((SWEEPS, 4)),
+            dma((3, 2)),
+            dma((3, 2)),
+            dma((BLOCKS, 8)),
+            dma((BLOCKS, 8)),
             dma((4,)),
             dma((4,)),
         ],
         compiler_params=pltpu.CompilerParams(
-            collective_id=0, has_side_effects=True, vmem_limit_bytes=24 * 2**20
+            collective_id=0, has_side_effects=True, vmem_limit_bytes=40 * 2**20
         ),
     )(mobility_table, state, initial, labels)
     return new_state[None]

time: 50.8 us -> 45 us (0.89)
  Pallas kernels: 46.4 us -> 40.5 us
    pallas_call x1, Pallas kernels: 46.4 us -> 40.5 us  [fused_shards(): pl.pallas_call(functools.partial(paradiag_kernel, slabs), out_shape=jax.S...]
where the time goes in v2:
time: 45 us; the launch traced here: 44.8 us
  Pallas kernels  40.5 us (90%)
  local copies, waits for them, and re-layouts  4.21 us (9%)
    pallas_call x1, Pallas kernels, fused_shards(): pl.pallas_call(functools.partial(paradiag_kernel, slabs), out_shape=jax.S...  40.5 us
    unnamed x9, local copies, waits for them, and re-layouts  4.21 us

profile of v2, /device:TPU:0, one launch (start us, length us, event | category | flops | bytes accessed | tf_op | source)
XLA Modules:
  0.0 44.8 jit_solution(10347025441481624732)
XLA Ops:
  0.0 0.0 copy-start
  0.0 0.9 %copy-done = f32[1,8,32,256]{3,2,1,0:T(8,128)S(1)} copy-done((f32[1,8,32,256]{3,2,1,0:T(8,128)S(1)}, f32[1,8,32,256]{3,2,1,0:T(8,128)}, u32[]{:S(2)}) %copy-start) | copy-done | bytes 262168
  1.0 0.0 copy-start.1
  1.0 0.9 %copy-done.1 = f32[8,32,256]{2,1,0:T(8,128)S(1)} copy-done((f32[8,32,256]{2,1,0:T(8,128)S(1)}, f32[8,32,256]{2,1,0:T(8,128)}, u32[]{:S(2)}) %copy-start.1) | copy-done | bytes 262168
  1.9 0.0 copy-start.2
  1.9 0.9 %copy-done.2 = s32[8,32,256]{2,1,0:T(8,128)S(1)} copy-done((s32[8,32,256]{2,1,0:T(8,128)S(1)}, s32[8,32,256]{2,1,0:T(8,128)}, u32[]{:S(2)}) %copy-start.2) | copy-done | bytes 262168
  2.9 0.0 copy-start.3
  2.9 0.7 %copy-done.3 = f32[16]{0:T(128)S(1)} copy-done((f32[16]{0:T(128)S(1)}, f32[16]{0:T(128)}, u32[]{:S(2)}) %copy-start.3) | copy-done | bytes 88
  3.5 40.5 %shard_map.46 = f32[8,32,256]{2,1,0:T(8,128)S(1)} custom-call(f32[16]{0:T(128)S(1)} %copy-done.3, f32[1,8,32,256]{3,2,1,0:T(8,128)S(1)} %copy-done, f32[8,32,256]{2,1,0:T(8,128)S(1)} %copy-done.1, s32[8,32,256]{2,1,0:T(8,128)S(1)} %copy-done.2), custom_call_target="tpu_custom_call" | custom-call | tf_op jit(solution)/shard_map/pallas_call | solution.py:542
  44.0 0.7 %copy.6 = f32[1,8,32,256]{3,2,1,0:T(8,128)} copy(f32[1,8,32,256]{3,2,1,0:T(8,128)S(1)} %bitcast.1) | data formatting | bytes 524288
Async XLA Ops:
  0.0 0.9 %copy-start = (f32[1,8,32,256]{3,2,1,0:T(8,128)S(1)}, f32[1,8,32,256]{3,2,1,0:T(8,128)}, u32[]{:S(2)}) copy-start(f32[1,8,32,256]{3,2,1,0:T(8,128)} %state_ref.1) | copy-start | bytes 786436
  1.0 0.9 %copy-start.1 = (f32[8,32,256]{2,1,0:T(8,128)S(1)}, f32[8,32,256]{2,1,0:T(8,128)}, u32[]{:S(2)}) copy-start(f32[8,32,256]{2,1,0:T(8,128)} %initial_ref.1) | copy-start | bytes 786436
  1.9 0.9 %copy-start.2 = (s32[8,32,256]{2,1,0:T(8,128)S(1)}, s32[8,32,256]{2,1,0:T(8,128)}, u32[]{:S(2)}) copy-start(s32[8,32,256]{2,1,0:T(8,128)} %labels_ref.1) | copy-start | bytes 786436
  2.9 0.7 %copy-start.3 = (f32[16]{0:T(128)S(1)}, f32[16]{0:T(128)}, u32[]{:S(2)}) copy-start(f32[16]{0:T(128)} %table_ref.1) | copy-start | bytes 196

commit v3 on v2

--- a/solution.py
+++ b/solution.py
@@ -186,6 +186,8 @@
     own_in,
     edges,
     edges_in,
+    corners,
+    corners_in,
     result,
     local_sem,
     a2a_send,
@@ -403,13 +405,13 @@
             )
         for side, other in enumerate((after, before)):
             moves.append(
-                (edges.at[block, side], edges_in.at[block, side, pl.ds(1, 2)], (other, s))
-            )
-            for slab, half, place in ((above, 1, 0), (below, 0, 3)):
+                (edges.at[block, side], edges_in.at[block, side], (other, s))
+            )
+            for slab, half, place in ((above, 1, 0), (below, 0, 1)):
                 moves.append(
                     (
-                        edges.at[block, side, half],
-                        edges_in.at[block, side, place],
+                        corners.at[block, side, half],
+                        corners_in.at[block, side, place],
                         (other, slab),
                     )
                 )
@@ -433,6 +435,12 @@
                     two = own[block, field, 4 * half + i + 2]
                     edges[block, 0, half, field, i] = jnp.where(upper, swap(one), two)
                     edges[block, 1, half, field, i] = jnp.where(upper, one, swap(two))
+            for half, nearest in enumerate(((0, 1, 2), (depth - 1, depth - 2, depth - 3))):
+                one, two, three = (own[block, field, z] for z in nearest)
+                two_three = jnp.where(row_number == 5, pltpu.roll(three, 6, 0), two)
+                corners[block, 0, half, field] = jnp.where(upper, swap(one), two_three)
+                two_three = jnp.where(row_number == 2, pltpu.roll(three, 2, 0), two)
+                corners[block, 1, half, field] = jnp.where(upper, two_three, swap(one))
             return carry
 
         lax.fori_loop(0, 4, of_field, 0)
@@ -448,10 +456,19 @@
                 else:
                     middle = own[block, field, z - HALO]
                 middle = swap(middle)
-                low = edges_in[block, 0, quarter, field, i]
-                high = edges_in[block, 1, quarter, field, i]
-                low = swap(low) if late else low
-                high = high if late else swap(high)
+                if quarter in (0, 3):
+                    away = HALO - z if quarter == 0 else z - HALO - depth + 1
+                    low = corners_in[block, 0, quarter // 3, field]
+                    high = corners_in[block, 1, quarter // 3, field]
+                    if away == 2:
+                        low, high = swap(low), swap(high)
+                    if away == 3:
+                        low, high = pltpu.roll(low, 6, 0), pltpu.roll(high, 2, 0)
+                else:
+                    low = edges_in[block, 0, quarter - 1, field, i]
+                    high = edges_in[block, 1, quarter - 1, field, i]
+                    low = swap(low) if late else low
+                    high = high if late else swap(high)
                 target[field, z, 0:8] = jnp.where(upper, low, middle)
                 target[field, z, 8:16] = jnp.where(upper, middle, high)
             return carry
@@ -542,7 +559,7 @@
     new_state = pl.pallas_call(
         functools.partial(paradiag_kernel, slabs),
         out_shape=jax.ShapeDtypeStruct((depth, rows, width), f32),
-        in_specs=[pl.BlockSpec(memory_space=pltpu.SMEM)] + [pl.BlockSpec(memory_space=pl.ANY)] * 3,
+        in_specs=[pl.BlockSpec(memory_space=pltpu.SMEM)] + [pl.BlockSpec(memory_space=pltpu.HBM)] * 3,
         out_specs=pl.BlockSpec(memory_space=pltpu.VMEM),
         scratch_shapes=[
             pltpu.VMEM((depth, rows, width), f32),
@@ -559,7 +576,9 @@
             pltpu.VMEM((BLOCKS + 1, 4, depth, 8, width), f32),
             pltpu.VMEM((BLOCKS, 2, 4, HALO, 8, width), f32),
             pltpu.VMEM((BLOCKS, 2, 2, 4, 2, 8, width), f32),
-            pltpu.VMEM((BLOCKS, 2, 4, 4, 2, 8, width), f32),
+            pltpu.VMEM((BLOCKS, 2, 2, 4, 2, 8, width), f32),
+            pltpu.VMEM((BLOCKS, 2, 2, 4, 8, width), f32),
+            pltpu.VMEM((BLOCKS, 2, 2, 4, 8, width), f32),
             pltpu.VMEM((4, depth, 8, width), f32),
             dma((9,)),
             dma((4,)),

time: 45 us -> 42.1 us (0.936)
  Pallas kernels: 40.5 us -> 37.7 us
    pallas_call x1, Pallas kernels: 40.5 us -> 37.7 us  [fused_shards(): pl.pallas_call(functools.partial(paradiag_kernel, slabs), out_shape=jax.S...]
where the time goes in v3:
time: 42.1 us; the launch traced here: 41.9 us
  Pallas kernels  37.7 us (90%)
  local copies, waits for them, and re-layouts  4.21 us (10%)
    pallas_call x1, Pallas kernels, fused_shards(): pl.pallas_call(functools.partial(paradiag_kernel, slabs), out_shape=jax.S...  37.7 us
    unnamed x9, local copies, waits for them, and re-layouts  4.21 us

profile of v3, /device:TPU:0, one launch (start us, length us, event | category | flops | bytes accessed | tf_op | source)
XLA Modules:
  0.0 41.9 jit_solution(591213762877946327)
XLA Ops:
  0.0 0.0 copy-start
  0.0 0.9 %copy-done = f32[1,8,32,256]{3,2,1,0:T(8,128)S(1)} copy-done((f32[1,8,32,256]{3,2,1,0:T(8,128)S(1)}, f32[1,8,32,256]{3,2,1,0:T(8,128)}, u32[]{:S(2)}) %copy-start) | copy-done | bytes 262168
  1.0 0.0 copy-start.1
  1.0 0.9 %copy-done.1 = f32[8,32,256]{2,1,0:T(8,128)S(1)} copy-done((f32[8,32,256]{2,1,0:T(8,128)S(1)}, f32[8,32,256]{2,1,0:T(8,128)}, u32[]{:S(2)}) %copy-start.1) | copy-done | bytes 262168
  1.9 0.0 copy-start.2
  1.9 0.9 %copy-done.2 = s32[8,32,256]{2,1,0:T(8,128)S(1)} copy-done((s32[8,32,256]{2,1,0:T(8,128)S(1)}, s32[8,32,256]{2,1,0:T(8,128)}, u32[]{:S(2)}) %copy-start.2) | copy-done | bytes 262168
  2.9 0.0 copy-start.3
  2.9 0.7 %copy-done.3 = f32[16]{0:T(128)S(1)} copy-done((f32[16]{0:T(128)S(1)}, f32[16]{0:T(128)}, u32[]{:S(2)}) %copy-start.3) | copy-done | bytes 88
  3.5 37.7 %shard_map.46 = f32[8,32,256]{2,1,0:T(8,128)S(1)} custom-call(f32[16]{0:T(128)S(1)} %copy-done.3, f32[1,8,32,256]{3,2,1,0:T(8,128)S(1)} %copy-done, f32[8,32,256]{2,1,0:T(8,128)S(1)} %copy-done.1, s32[8,32,256]{2,1,0:T(8,128)S(1)} %copy-done.2), custom_call_target="tpu_custom_call" | custom-call | tf_op jit(solution)/shard_map/pallas_call | solution.py:559
  41.2 0.7 %copy.6 = f32[1,8,32,256]{3,2,1,0:T(8,128)} copy(f32[1,8,32,256]{3,2,1,0:T(8,128)S(1)} %bitcast.1) | data formatting | bytes 524288
Async XLA Ops:
  0.0 0.9 %copy-start = (f32[1,8,32,256]{3,2,1,0:T(8,128)S(1)}, f32[1,8,32,256]{3,2,1,0:T(8,128)}, u32[]{:S(2)}) copy-start(f32[1,8,32,256]{3,2,1,0:T(8,128)} %state_ref.1) | copy-start | bytes 786436
  1.0 0.9 %copy-start.1 = (f32[8,32,256]{2,1,0:T(8,128)S(1)}, f32[8,32,256]{2,1,0:T(8,128)}, u32[]{:S(2)}) copy-start(f32[8,32,256]{2,1,0:T(8,128)} %initial_ref.1) | copy-start | bytes 786436
  1.9 0.9 %copy-start.2 = (s32[8,32,256]{2,1,0:T(8,128)S(1)}, s32[8,32,256]{2,1,0:T(8,128)}, u32[]{:S(2)}) copy-start(s32[8,32,256]{2,1,0:T(8,128)} %labels_ref.1) | copy-start | bytes 786436
  2.9 0.7 %copy-start.3 = (f32[16]{0:T(128)S(1)}, f32[16]{0:T(128)}, u32[]{:S(2)}) copy-start(f32[16]{0:T(128)} %table_ref.1) | copy-start | bytes 196

commit v4 on v3

--- a/solution.py
+++ b/solution.py
@@ -595,7 +595,7 @@
             dma((4,)),
         ],
         compiler_params=pltpu.CompilerParams(
-            collective_id=0, has_side_effects=True, vmem_limit_bytes=40 * 2**20
+            collective_id=0, has_side_effects=True, vmem_limit_bytes=60 * 2**20
         ),
     )(mobility_table, state, initial, labels)
     return new_state[None]

time: 42.1 us -> 40.3 us (0.957)
  local copies, waits for them, and re-layouts: 4.21 us -> 1.67 us
  Pallas kernels: 37.7 us -> 38.5 us
    unnamed x9 -> x1, local copies, waits for them, and re-layouts: 4.21 us -> 1.67 us
    pallas_call x1, Pallas kernels: 37.7 us -> 38.5 us  [fused_shards(): pl.pallas_call(functools.partial(paradiag_kernel, slabs), out_shape=jax.S...]
where the time goes in v4:
time: 40.3 us; the launch traced here: 40.2 us
  Pallas kernels  38.5 us (96%)
  local copies, waits for them, and re-layouts  1.67 us (4%)
    pallas_call x1, Pallas kernels, fused_shards(): pl.pallas_call(functools.partial(paradiag_kernel, slabs), out_shape=jax.S...  38.5 us
    unnamed x1, local copies, waits for them, and re-layouts  1.67 us

profile of v4, /device:TPU:0, one launch (start us, length us, event | category | flops | bytes accessed | tf_op | source)
XLA Modules:
  0.0 40.2 jit_solution(17939054291900054487)
XLA Ops:
  0.0 38.5 %shard_map.46 = f32[8,32,256]{2,1,0:T(8,128)} custom-call(f32[16]{0:T(128)} %table_ref.1, f32[1,8,32,256]{3,2,1,0:T(8,128)} %state_ref.1, f32[8,32,256]{2,1,0:T(8,128)} %initial_ref.1, s32[8,32,256]{2,1,0:T(8,128)} %labels_ref.1), custom_call_target="tpu_custom_call" | custom-call | tf_op jit(solution)/shard_map/pallas_call | solution.py:559
  38.5 1.7 %copy.6 = f32[1,8,32,256]{3,2,1,0:T(8,128)} copy(f32[1,8,32,256]{3,2,1,0:T(8,128)} %bitcast.1) | data formatting | bytes 524288

commit v5 on v4

--- a/solution.py
+++ b/solution.py
@@ -243,14 +243,6 @@
     load_first = pltpu.make_async_copy(initial_ref.at[:, my_rows, :], first, local_sem.at[3])
     load_first.start()
 
-    load_home.wait()
-    for place in range(4):
-        for side, row in enumerate(((8 * place + 31) % 32, (8 * place + 8) % 32)):
-            for z in range(depth):
-                rows_out[place, side, z : z + 1, :] = home[z, row : row + 1, :]
-    load_rows = pltpu.make_async_copy(rows_out.at[p], rows_in.at[t], local_sem.at[4])
-    load_rows.start()
-
     pl.semaphore_wait(barrier, 11)
 
     sends = []
@@ -260,7 +252,7 @@
         other_rows = pl.ds(pl.multiple_of(place * 8, 8), 8)
         sends.append(
             pltpu.make_async_remote_copy(
-                src_ref=home.at[:, other_rows, :],
+                src_ref=state_ref.at[0, :, other_rows, :],
                 dst_ref=chunk.at[t],
                 send_sem=a2a_send.at[ahead],
                 recv_sem=a2a_recv.at[4 - ahead],
@@ -285,7 +277,7 @@
         for side, (slab, plane) in enumerate(((above, depth - 1), (below, 0))):
             sends.append(
                 pltpu.make_async_remote_copy(
-                    src_ref=home.at[plane, other_rows, :],
+                    src_ref=state_ref.at[0, plane, other_rows, :],
                     dst_ref=planes_in.at[t, side],
                     send_sem=planes_send.at[ahead, side],
                     recv_sem=planes_recv.at[(4 - ahead) % 4, side],
@@ -308,7 +300,17 @@
                     device_id_type=MESH,
                 )
             )
-    for copy in sends + class_sends:
+    row_sends = sends[1:6:2]
+    for copy in sends[0:6:2]:
+        copy.start()
+    load_home.wait()
+    for place in range(4):
+        for side, row in enumerate(((8 * place + 31) % 32, (8 * place + 8) % 32)):
+            for z in range(depth):
+                rows_out[place, side, z : z + 1, :] = home[z, row : row + 1, :]
+    load_rows = pltpu.make_async_copy(rows_out.at[p], rows_in.at[t], local_sem.at[4])
+    load_rows.start()
+    for copy in row_sends + sends[6:] + class_sends:
         copy.start()
 
     row_number = lax.broadcasted_iota(jnp.int32, (8, width), 0)

time: 40.3 us -> 40.5 us (level)
  no operation moved by 1% of the time
where the time goes in v5:
time: 40.5 us; the launch traced here: 40.4 us
  Pallas kernels  38.7 us (96%)
  local copies, waits for them, and re-layouts  1.67 us (4%)
    pallas_call x1, Pallas kernels, fused_shards(): pl.pallas_call(functools.partial(paradiag_kernel, slabs), out_shape=jax.S...  38.7 us
    unnamed x1, local copies, waits for them, and re-layouts  1.67 us

profile of v5, /device:TPU:0, one launch (start us, length us, event | category | flops | bytes accessed | tf_op | source)
XLA Modules:
  0.0 40.4 jit_solution(13064863009061738064)
XLA Ops:
  0.0 38.7 %shard_map.46 = f32[8,32,256]{2,1,0:T(8,128)} custom-call(f32[16]{0:T(128)} %table_ref.1, f32[1,8,32,256]{3,2,1,0:T(8,128)} %state_ref.1, f32[8,32,256]{2,1,0:T(8,128)} %initial_ref.1, s32[8,32,256]{2,1,0:T(8,128)} %labels_ref.1), custom_call_target="tpu_custom_call" | custom-call | tf_op jit(solution)/shard_map/pallas_call | solution.py:561
  38.7 1.7 %copy.6 = f32[1,8,32,256]{3,2,1,0:T(8,128)} copy(f32[1,8,32,256]{3,2,1,0:T(8,128)} %bitcast.1) | data formatting | bytes 524288

commit v6 on v4

--- a/solution.py
+++ b/solution.py
@@ -496,11 +496,13 @@
 
     halos = []
     for block in range(BLOCKS):
-        put_edges(block)
         copies = block_copies(block)
         halos += copies
-        for copy in copies:
+        for copy in copies[:2]:
             copy.start()
+        put_edges(block)
+        for number in (3, 4, 6, 7, 2, 5):
+            copies[number].start()
         for copy in copies:
             copy.wait_recv()
         source = base if block == 0 else sol.at[0]

time: 40.3 us -> 40.5 us (level)
  no operation moved by 1% of the time
where the time goes in v6:
time: 40.5 us; the launch traced here: 40.3 us
  Pallas kernels  38.6 us (95%)
  local copies, waits for them, and re-layouts  1.67 us (4%)
    pallas_call x1, Pallas kernels, fused_shards(): pl.pallas_call(functools.partial(paradiag_kernel, slabs), out_shape=jax.S...  38.6 us
    unnamed x1, local copies, waits for them, and re-layouts  1.67 us

profile of v6, /device:TPU:0, one launch (start us, length us, event | category | flops | bytes accessed | tf_op | source)
XLA Modules:
  0.0 40.3 jit_solution(13925499122161525815)
XLA Ops:
  0.0 38.6 %shard_map.46 = f32[8,32,256]{2,1,0:T(8,128)} custom-call(f32[16]{0:T(128)} %table_ref.1, f32[1,8,32,256]{3,2,1,0:T(8,128)} %state_ref.1, f32[8,32,256]{2,1,0:T(8,128)} %initial_ref.1, s32[8,32,256]{2,1,0:T(8,128)} %labels_ref.1), custom_call_target="tpu_custom_call" | custom-call | tf_op jit(solution)/shard_map/pallas_call | solution.py:561
  38.6 1.7 %copy.6 = f32[1,8,32,256]{3,2,1,0:T(8,128)} copy(f32[1,8,32,256]{3,2,1,0:T(8,128)} %bitcast.1) | data formatting | bytes 524288
